TPU v7x, 128 devices: a whole 4x4x4 slice. The times are simulated.
128 devices in a mesh: pool: 2 (over y_hi), dom: 32 (over x, z, core), band: 2 (over y_lo).
Axes of the slice: x: 4, y: 4 (y_hi: 2, y_lo: 2; y = y_hi * 2 + y_lo), z: 4, core: 2. Of those that a mesh axis runs over, the one named last changes fastest.
Arguments:
- states_in: float32 [2, 32, 128, 19200], P('pool', 'dom', 'band'), may hold values from -6 to 6
- bloch_flip: int32 [2, 3], P('pool'), may hold values from 0 to 1
- kweight_num: int32 [2], P('pool'), may hold values from 1 to 7
- local_pot: float32 [32, 19200], P('dom'), may hold values from -1 to 1
- proj_values: float32 [32, 64, 19200], P('dom'), may hold values from -0.046875 to 0.046875
- proj_ids: int32 [32, 64], P('dom'), may hold values from 0 to 511, all different within a row
- coupling: float32 [512], replicated, may hold values from 0.5 to 2
- occupation: float32 [128], P('band'), may hold values from 0.5 to 2
Outputs:
- filtered: float32 [2, 32, 128, 19200], P('pool', 'dom', 'band')
- density: float32 [32, 19200], P('dom', ('pool', 'band'))
Inputs may be any that keep to these rules, and one draw needn't show every extreme that they name: `proj_ids`: each box names 64 different projectors, and every projector is named by some box.
All inputs are finite; a program needn't handle non-finite values.
Results may differ from a plain program's by a relative error of at most 0.0001.
Values sent between devices are 32-bit elements; how exact they have to be, the bound alone decides.
A program may use at most 256 MiB of HBM per device.

v0:
```python
import jax
import jax.numpy as jnp
from jax import lax
from jax.sharding import PartitionSpec as P

HALO = 6
CX = 24
CY = 20
CZ = 40


COEFFS = (
    -5369.0 / 1800.0,
    12.0 / 7.0,
    -15.0 / 56.0,
    10.0 / 189.0,
    -1.0 / 112.0,
    2.0 / 1925.0,
    -1.0 / 16632.0,
)
CENTER = 14.0
HALF_WIDTH = 10.0


def partner(value, axis, bit):
    mask = 2**bit
    pairs = [(source, source ^ mask) for source in range(lax.axis_size(axis))]
    return lax.ppermute(value, axis, pairs)


def neighbour(send, bit):
    return partner(send, "dom", bit)


def faces_of(field, dim, first_bit, nbits, sign, index):
    width = field.shape[dim]
    top = lax.slice_in_dim(field, width - HALO, width, axis=dim)
    bottom = lax.slice_in_dim(field, 0, HALO, axis=dim)
    if nbits == 1:
        place = index >> first_bit & 1
        got = neighbour(jnp.concatenate([top, bottom], axis=dim), first_bit)
        lower = lax.slice_in_dim(got, 0, HALO, axis=dim) * jnp.where(place == 0, sign, 1.0)
        upper = lax.slice_in_dim(got, HALO, 2 * HALO, axis=dim) * jnp.where(place == 1, sign, 1.0)
    else:
        code = index >> first_bit & 3
        place = code ^ code >> 1
        even = place % 2 == 0
        got_low = neighbour(jnp.where(even, top, bottom), first_bit)
        got_high = neighbour(jnp.where(even, bottom, top), first_bit + 1)
        upper = jnp.where(even, got_low, got_high) * jnp.where(place == 3, sign, 1.0)
        lower = jnp.where(even, got_high, got_low) * jnp.where(place == 0, sign, 1.0)
    return (lower, upper)


def second_diff(ext, dim, width):
    acc = COEFFS[0] * lax.slice_in_dim(ext, HALO, HALO + width, axis=dim)
    for shift in range(1, HALO + 1):
        acc = acc + COEFFS[shift] * (
            lax.slice_in_dim(ext, HALO + shift, HALO + shift + width, axis=dim)
            + lax.slice_in_dim(ext, HALO - shift, HALO - shift + width, axis=dim)
        )
    return acc


def direction_term(field, dim, first_bit, nbits, sign, index):
    width = field.shape[dim]
    lower, upper = faces_of(field, dim, first_bit, nbits, sign, index)
    return second_diff(jnp.concatenate([lower, field, upper], axis=dim), dim, width)


def body(
    states_in, bloch_flip, kweight_num, local_pot, proj_values, proj_ids, coupling, occupation
):
    index = lax.axis_index("dom")
    dom_count = lax.axis_size("dom")
    boxes_y = min(4, dom_count // 4)
    boxes_x = dom_count // (2 * boxes_y)
    ybits = boxes_y.bit_length() - 1
    xbits = boxes_x.bit_length() - 1
    signs = 1.0 - 2.0 * bloch_flip[0].astype(jnp.float32)
    states_dev = states_in.shape[2]
    cells = states_in.shape[3]
    start = states_in[0, 0].reshape(states_dev, CX, CY, CZ)
    potential = local_pot[0].reshape(CX, CY, CZ)
    proj_flat = proj_values[0]
    nproj_all = coupling.shape[0]
    onehot = (proj_ids[0][:, None] == jnp.arange(nproj_all, dtype=jnp.int32)[None, :]).astype(
        jnp.float32
    )
    highest = lax.Precision.HIGHEST

    def hamilton(field):
        lap_x = direction_term(field, 1, 1 + ybits, xbits, signs[0], index)
        lap_y = direction_term(field, 2, 1, ybits, signs[1], index)
        lap_z = direction_term(field, 3, 0, 1, signs[2], index)
        lap = lap_x + lap_y + lap_z
        flat = field.reshape(states_dev, cells)
        coef = lax.dot_general(flat, proj_flat, (((1,), (1,)), ((), ())), precision=highest)
        partial_sums = jnp.dot(coef, onehot, precision=highest)
        total = lax.psum(partial_sums, "dom")
        scaled = total * coupling[None, :]
        back = lax.dot_general(scaled, onehot, (((1,), (1,)), ((), ())), precision=highest)
        nonlocal_part = jnp.dot(back, proj_flat, precision=highest).reshape(field.shape)
        return -0.5 * lap + potential[None] * field + nonlocal_part

    first = (hamilton(start) - CENTER * start) / HALF_WIDTH
    second = 2.0 * (hamilton(first) - CENTER * first) / HALF_WIDTH - start
    second_flat = second.reshape(states_dev, cells)
    numer = kweight_num.astype(jnp.float32)
    total_num = lax.psum(numer, "pool")
    own = jnp.sum(occupation[:, None] * second_flat * second_flat, axis=0) * numer[0]
    summed = lax.psum_scatter(own[None], ("pool", "band"), scatter_dimension=1, tiled=True)
    return (second_flat[None, None], summed / total_num[0])


def solution(mesh):
    placed = (
        P("pool", "dom", "band", None),
        P("pool", None),
        P("pool"),
        P("dom", None),
        P("dom", None, None),
        P("dom", None),
        P(),
        P("band"),
    )
    return jax.shard_map(
        body,
        mesh=mesh,
        in_specs=placed,
        out_specs=(P("pool", "dom", "band", None), P("dom", ("pool", "band"))),
        check_vma=False,
    )
```

profile of v0, /device:TPU:0, one launch (start us, length us, event | category | flops | bytes accessed | tf_op | source)
XLA Modules:
  0.0 817.4 jit_solution(16640150304570412870)
XLA Ops:
  7.2 8.1 copy.17
  15.4 5.6 slice_select_fusion.3
  23.0 3.6 collective-permute-start.3
  26.6 5.0 slice_select_fusion.7
  39.1 3.3 copy.18
  42.5 4.0 fusion.185
  49.1 8.1 copy.21
  62.3 127.5 %all-reduce.3.cloned.1.call-done = f32[64,512]{1,0:T(8,128)} async-done(((f32[64,512]{1,0:T(8,128)}), f32[64,512]{1,0:T(8,128)}) %all-reduce.3.cloned.1.call-update) | async-done | bytes 131088 | tf_op jit(solution)/shard_map/psum | solution.py:100
  191.0 5.2 select_multiply_fusion.7
  200.8 4.9 select_multiply_fusion.3
  205.7 160.3 %broadcast_multiply_fusion = (f32[64,24,20,40]{0,3,2,1:T(8,128)}, f32[64,24,20,40]{0,3,2,1:T(8,128)}) fusion(f32[64,24,20,40]{0,3,2,1:T(8,128)} %bitcast.42, f32[64,64,1,1]{1,0,3,2:T(8,128)S(1)} %convolution_bitcast_fusion.1, f32[24,20,40,64]{3,2,1,0:T(8,128)} %bitcast.52, f32[24,20,40]{2,1,0:T(8,128)S(1)} %mul.298, ...), kind=kOutput, calls=%fused_computation.321 | convolution fusion | flops 1066598400 | bytes 26635264 | tf_op jit(solution)/shard_map/dot_general | solution.py:103
  366.0 5.5 slice_select_fusion.5
  374.4 3.9 collective-permute-start.6
  379.0 3.3 copy.22
  382.5 15.8 %fusion.183 = f32[64,64]{1,0:T(8,128)S(1)} fusion(f32[64,19200]{0,1:T(8,128)S(1)} %bitcast.44, f32[1,64,19200]{2,1,0:T(8,128)S(1)} %bitcast.48), kind=kOutput, calls=%fused_computation.316 | convolution fusion | flops 943718400 | bytes 9846784 | tf_op jit(solution)/shard_map/dot_general | solution.py:98
  399.3 5.7 slice_select_fusion.1
  406.7 128.5 %all-reduce.5.cloned.1.call-done = f32[64,512]{1,0:T(8,128)} async-done(((f32[64,512]{1,0:T(8,128)}), f32[64,512]{1,0:T(8,128)}) %all-reduce.5.cloned.1.call-update) | async-done | bytes 131088 | tf_op jit(solution)/shard_map/psum | solution.py:100
  536.4 5.2 select_multiply_fusion.5
  546.9 4.8 select_multiply_fusion.1
  551.8 158.6 %fusion.118 = (f32[24,20,40]{2,1,0:T(8,128)S(1)}, f32[64,24,20,40]{0,3,2,1:T(8,128)}) fusion(f32[64]{0:T(128)S(1)} %copy-done.6, f32[64,24,20,40]{0,3,2,1:T(8,128)} %bitcast.43, f32[64,24,20,40]{0,3,2,1:T(8,128)} %get-tuple-element.36, f32[64,64,1,1]{1,0,3,2:T(8,128)S(1)} %convolution_bitcast_fusion, f32[24,20,40,64]{3,2,1,0:T(8,128)} %bitcast.53, ...), kind=kOutput, calls=%fused_computation.239 | convolution fusion | flops 1071494400 | bytes 31627520 | tf_op jit(solution)/shard_map/dot_general | solution.py:103
  710.4 5.2 mul.344
  715.6 7.6 psum.23
  723.2 9.2 %copy.25 = f32[1,1,64,19200]{3,2,1,0:T(8,128)} copy(f32[1,1,64,19200]{2,3,1,0:T(8,128)} %bitcast.54) | data formatting | bytes 9830400
  732.4 74.5 %reduce-scatter.4.cloned.1.call-done = f32[4800,1]{1,0:T(8,128)} async-done(((f32[19200,1]{1,0:T(8,128)}), f32[4800,1]{1,0:T(8,128)}) %reduce-scatter.4.cloned.1.call-update) | async-done | bytes 19216
  (74 shorter events, 35.1 us)
Async XLA Ops:
  7.2 182.6 %all-reduce.3.cloned.1.call-start = ((), (), s32[]{:S(2)}) async-start(), calls=%async_computation.1 | async-start | bytes 262144 | tf_op jit(solution)/shard_map/psum | solution.py:100
  21.0 179.8 %collective-permute-start.2 = (f32[64,24,6,40]{0,3,2,1:T(8,128)}, f32[64,24,6,40]{0,3,2,1:T(8,128)S(1)}, u32[]{:S(2)}, u32[]{:S(2)}) collective-permute-start(f32[64,24,6,40]{0,3,2,1:T(8,128)} %get-tuple-element.14), channel_id=1, source_target_pairs={{0,4},{2,6},{4,0},{6,2},{8,12},{10,14},{12,8},{14,10},{16,20},{18,... | collective-permute-start | bytes 4423688 | tf_op jit(solution)/shard_map/ppermute | solution.py:28
  23.0 177.8 %collective-permute-start.3 = (f32[64,24,6,40]{0,3,2,1:T(8,128)}, f32[64,24,6,40]{0,3,2,1:T(8,128)}, u32[]{:S(2)}, u32[]{:S(2)}) collective-permute-start(f32[64,24,6,40]{0,3,2,1:T(8,128)} %get-tuple-element.15), channel_id=1, source_target_pairs={{0,8},{2,10},{4,12},{6,14},{8,0},{10,2},{12,4},{14,6},{16,24},{18,... | collective-permute-start | bytes 4423688 | tf_op jit(solution)/shard_map/ppermute | solution.py:28
  31.6 159.4 %collective-permute-start = (f32[64,6,20,40]{0,3,2,1:T(8,128)}, f32[64,6,20,40]{0,3,2,1:T(8,128)}, u32[]{:S(2)}, u32[]{:S(2)}) collective-permute-start(f32[64,6,20,40]{0,3,2,1:T(8,128)} %get-tuple-element.16), channel_id=1, source_target_pairs={{0,16},{2,18},{4,20},{6,22},{8,24},{10,26},{12,28},{14,30},{16,0},... | collective-permute-start | bytes 3686408 | tf_op jit(solution)/shard_map/ppermute | solution.py:28
  33.1 9.3 %slice-start = ((s8[4915200]{0:T(1024)(128)(4,1)}), s8[4194304]{0:T(1024)(128)(4,1)S(1)}, s32[]{:S(2)}) async-start(s8[4915200]{0:T(1024)(128)(4,1)} %bitcast.45), calls=%async_computation.4 | async-start | bytes 8388608
  33.1 9.3 %slice-start.4 = ((s8[4915200]{0:T(1024)(128)(4,1)}), s8[4194304]{0:T(1024)(128)(4,1)S(1)}, s32[]{:S(2)}) async-start(s8[4915200]{0:T(1024)(128)(4,1)} %bitcast.50), calls=%async_computation.8 | async-start | bytes 8388608
  33.1 157.9 %collective-permute-start.1 = (f32[64,6,20,40]{0,3,2,1:T(8,128)}, f32[64,6,20,40]{0,3,2,1:T(8,128)}, u32[]{:S(2)}, u32[]{:S(2)}) collective-permute-start(f32[64,6,20,40]{0,3,2,1:T(8,128)} %get-tuple-element.17), channel_id=1, source_target_pairs={{0,32},{2,34},{4,36},{6,38},{8,40},{10,42},{12,44},{14,46},{16,48}... | collective-permute-start | bytes 3686408 | tf_op jit(solution)/shard_map/ppermute | solution.py:28
  39.1 7.4 copy-start.3
  39.1 8.9 %copy-start.2 = (f32[1,19200]{1,0:T(1,128)S(1)}, f32[1,19200]{1,0:T(1,128)}, u32[]{:S(2)}) copy-start(f32[1,19200]{1,0:T(1,128)} %param.11) | copy-start | bytes 230404
  39.1 10.0 %copy-start.5 = (s32[1,3]{1,0:T(1,128)S(1)}, s32[1,3]{1,0:T(1,128)}, u32[]{:S(2)}) copy-start(s32[1,3]{1,0:T(1,128)} %param.9) | copy-start | bytes 40
  42.4 153.8 %collective-permute-start.4 = (f32[64,24,20,12]{0,1,3,2:T(8,128)}, f32[64,24,20,12]{0,1,3,2:T(8,128)}, u32[]{:S(2)}, u32[]{:S(2)}) collective-permute-start(f32[64,24,20,12]{0,1,3,2:T(8,128)} %copy.18), channel_id=1, source_target_pairs={{0,2},{2,0},{4,6},{6,4},{8,10},{10,8},{12,14},{14,12},{16,18},{18,... | collective-permute-start | bytes 4423688 | tf_op jit(solution)/shard_map/ppermute | solution.py:28
  46.5 143.3 %copy-start.4 = (f32[512]{0:T(512)S(1)}, f32[512]{0:T(512)}, u32[]{:S(2)}) copy-start(f32[512]{0:T(512)} %param.14) | copy-start | bytes 6148
  47.5 487.7 %all-reduce.5.cloned.1.call-start = ((), (), s32[]{:S(2)}) async-start(), calls=%async_computation.2 | async-start | bytes 262144 | tf_op jit(solution)/shard_map/psum | solution.py:100
  366.0 7.0 copy-start
  373.1 9.5 %slice-start.2 = ((s8[4915200]{0:T(1024)(128)(4,1)}), s8[4194304]{0:T(1024)(128)(4,1)S(1)}, s32[]{:S(2)}) async-start(s8[4915200]{0:T(1024)(128)(4,1)} %bitcast.47), calls=%async_computation.6 | async-start | bytes 8388608
  373.4 162.9 %collective-permute-start.5 = (f32[64,6,20,40]{0,3,2,1:T(8,128)}, f32[64,6,20,40]{0,3,2,1:T(8,128)}, u32[]{:S(2)}, u32[]{:S(2)}) collective-permute-start(f32[64,6,20,40]{0,3,2,1:T(8,128)} %get-tuple-element.10), channel_id=1, source_target_pairs={{0,16},{2,18},{4,20},{6,22},{8,24},{10,26},{12,28},{14,30},{16,0},... | collective-permute-start | bytes 3686408 | tf_op jit(solution)/shard_map/ppermute | solution.py:28
  374.4 162.0 %collective-permute-start.6 = (f32[64,6,20,40]{0,3,2,1:T(8,128)}, f32[64,6,20,40]{0,3,2,1:T(8,128)}, u32[]{:S(2)}, u32[]{:S(2)}) collective-permute-start(f32[64,6,20,40]{0,3,2,1:T(8,128)} %get-tuple-element.11), channel_id=1, source_target_pairs={{0,32},{2,34},{4,36},{6,38},{8,40},{10,42},{12,44},{14,46},{16,48}... | collective-permute-start | bytes 3686408 | tf_op jit(solution)/shard_map/ppermute | solution.py:28
  378.3 4.2 slice-start.3
  382.3 159.2 %collective-permute-start.9 = (f32[64,24,20,12]{0,1,3,2:T(8,128)}, f32[64,24,20,12]{0,1,3,2:T(8,128)}, u32[]{:S(2)}, u32[]{:S(2)}) collective-permute-start(f32[64,24,20,12]{0,1,3,2:T(8,128)} %copy.22), channel_id=1, source_target_pairs={{0,2},{2,0},{4,6},{6,4},{8,10},{10,8},{12,14},{14,12},{16,18},{18,... | collective-permute-start | bytes 4423688 | tf_op jit(solution)/shard_map/ppermute | solution.py:28
  399.3 407.7 %reduce-scatter.4.cloned.1.call-start = ((), (), s32[]{:S(2)}) async-start(), calls=%async_computation.3 | async-start | bytes 12288000
  405.0 142.0 %collective-permute-start.7 = (f32[64,24,6,40]{0,3,2,1:T(8,128)}, f32[64,24,6,40]{0,3,2,1:T(8,128)S(1)}, u32[]{:S(2)}, u32[]{:S(2)}) collective-permute-start(f32[64,24,6,40]{0,3,2,1:T(8,128)} %get-tuple-element.8), channel_id=1, source_target_pairs={{0,4},{2,6},{4,0},{6,2},{8,12},{10,14},{12,8},{14,10},{16,20},{18,... | collective-permute-start | bytes 4423688 | tf_op jit(solution)/shard_map/ppermute | solution.py:28
  405.0 142.0 %collective-permute-start.8 = (f32[64,24,6,40]{0,3,2,1:T(8,128)}, f32[64,24,6,40]{0,3,2,1:T(8,128)}, u32[]{:S(2)}, u32[]{:S(2)}) collective-permute-start(f32[64,24,6,40]{0,3,2,1:T(8,128)} %get-tuple-element.9), channel_id=1, source_target_pairs={{0,8},{2,10},{4,12},{6,14},{8,0},{10,2},{12,4},{14,6},{16,24},{18,... | collective-permute-start | bytes 4423688 | tf_op jit(solution)/shard_map/ppermute | solution.py:28
  543.6 8.2 %copy-start.1 = (f32[24,20,40]{2,1,0:T(8,128)S(1)}, f32[24,20,40]{2,1,0:T(8,128)}, u32[]{:S(2)}) copy-start(f32[24,20,40]{2,1,0:T(8,128)} %broadcast_multiply_fusion.2) | copy-start | bytes 230404
  543.6 8.2 %copy-start.6 = (f32[64]{0:T(128)S(1)}, f32[64]{0:T(128)}, u32[]{:S(2)}) copy-start(f32[64]{0:T(128)} %param.15) | copy-start | bytes 772
  (2 other events, 8.2 us)
Sparse Core Ops, SparseCore 0:
  47.6 142.1 all-reduce.2
  399.4 135.7 all-reduce.4
  715.7 91.1 reduce-scatter.3
where the time goes:
time: 826 us; the launch traced here: 817 us
  matrix products  343 us (42%)
  waiting for transfers between devices  331 us (40%)
  other arithmetic  51.5 us (6%)
  local copies, waits for them, and re-layouts  48.8 us (6%)
  between operations  18.8 us (2%)
  starting transfers between devices  17.2 us (2%)
    dot_general x2, matrix products, hamilton(): jnp.dot(back, proj_flat, precision=highest).reshape(field.shape)  319 us
    psum x2, waiting for transfers between devices, hamilton(): total = lax.psum(partial_sums, 'dom')  256 us
    unnamed x4, waiting for transfers between devices  74.6 us
    unnamed x30, local copies, waits for them, and re-layouts  29.4 us
    select_n x4, other arithmetic, faces_of(): got_low = neighbour(jnp.where(even, top, bottom), first_bit)  21.8 us
    mul x4, other arithmetic, faces_of(): jnp.where(even, got_low, got_high) * jnp.where(place == 3, sign, 1.0)  20.1 us
    dot_general x2, matrix products, hamilton(): lax.dot_general(flat, proj_flat, (((1,), (1,)), ((), ())), precision=high...  19.8 us
    ppermute x10, starting transfers between devices, partner(): return lax.ppermute(value, axis, pairs)  16.6 us
  transfers between devices with their start and end apart: 13, of which 3 were waited for; matrix products, arithmetic and copies ran while one was open for 10% of the time, Pallas kernels for 0%

commit v1 on v0

v1 whole, which is shorter than its diff:
```python
import jax
import jax.numpy as jnp
import numpy as np
from jax import lax
from jax.experimental import pallas as pl
from jax.experimental.pallas import tpu as pltpu
from jax.sharding import PartitionSpec as P

MESH = pl.DeviceIdType.MESH
F32 = jnp.float32
BF16 = jnp.bfloat16

HALO = 6
CX = 24
CY = 20
CZ = 40
CELLS = CX * CY * CZ
COEFFS = (
    -5369.0 / 1800.0,
    12.0 / 7.0,
    -15.0 / 56.0,
    10.0 / 189.0,
    -1.0 / 112.0,
    2.0 / 1925.0,
    -1.0 / 16632.0,
)
CENTER = 14.0
HALF_WIDTH = 10.0
SCALE = -0.5 / HALF_WIDTH

GROUPS = 3
XL = CX // GROUPS
ROWS = XL * CY
USED = GROUPS * CZ
THIRD = CELLS // GROUPS
BLOCKS = 10
LINES = 16
STATES = 64
CH = 8
SLOTS = 64
PAIRS = ROWS // 2
YROWS = 45
XROWS = 40
PIECE = 4864
NOTE = PIECE + 128

Y_MASKS = (2, 4, 6)
X_MASKS = (8, 16, 24)
ALL_MASKS = (1,) + Y_MASKS + X_MASKS


def z_matrices():
    own = np.zeros((128, 128), np.float64)
    low = np.zeros((128, 128), np.float64)
    up = np.zeros((128, 128), np.float64)
    for group in range(GROUPS):
        for z in range(CZ):
            for shift in range(1, HALO + 1):
                for source in (z + shift, z - shift):
                    target = own if 0 <= source < CZ else (low if source < 0 else up)
                    target[group * CZ + source % CZ, group * CZ + z] += SCALE * COEFFS[shift]
    pairs = []
    for matrix in (own, low, up):
        high = jnp.asarray(matrix, F32).astype(BF16)
        rest = (jnp.asarray(matrix, F32) - high.astype(F32)).astype(BF16)
        pairs.append(jnp.concatenate([high, rest], axis=1))
    return pairs


def flip_bits(me, mask):
    other = me
    for bit in (1, 2, 4, 8, 16):
        if mask & bit:
            other = other + bit * (1 - 2 * ((me // bit) % 2))
    return other


def lanes_of(rows):
    return lax.broadcasted_iota(jnp.int32, (rows, 128), 1)


def roll(value, shift):
    shift = shift % 128
    if shift == 0:
        return value
    return pltpu.roll(value, shift, value.ndim - 1)


def split(value):
    high = value.astype(BF16)
    return high, (value - high.astype(F32)).astype(BF16)


def rows_from_lines(load, count, put):
    lane = lanes_of(count)
    tiles = [[load(group, tile) for tile in range(5)] for group in range(GROUPS)]
    for line in range(LINES):
        tile, offset = divmod(CZ * line, 128)
        parts = []
        for group in range(GROUPS):
            value = tiles[group][tile]
            if offset + CZ > 128:
                value = jnp.where(lane >= offset, value, tiles[group][tile + 1])
            parts.append(roll(value, CZ * group - offset))
        row = jnp.where(lane < CZ, parts[0], jnp.where(lane < 2 * CZ, parts[1], parts[2]))
        put(line, jnp.where(lane < USED, row, 0.0))


def lines_from_rows(rows, put):
    lane = lanes_of(8)
    for group in range(GROUPS):
        for tile in range(5):
            first, offset = divmod(128 * tile, CZ)
            value = None
            for step in range(4):
                part = roll(rows[first + step], CZ * step - offset - CZ * group)
                value = part if step == 0 else jnp.where(lane < CZ * step - offset, value, part)
            put(group, tile, value)


def kernel(
    states,
    flips,
    numer,
    pot,
    proj,
    ids,
    coupling,
    occupation,
    k_own,
    k_low,
    k_up,
    out,
    dens,
    cur,
    nxt,
    nonloc,
    pbox,
    send_y,
    send_x,
    recv_y,
    recv_x,
    recv_z,
    ext_x,
    ext_y,
    potential,
    kz,
    gather1,
    gather2,
    same,
    occ_rows,
    square,
    rho,
    notes,
    got_notes,
    stage_in,
    stage_out,
    in_sem,
    out_sem,
    send_sem,
    recv_sem,
    gsend_sem,
    grecv_sem,
    nsend_sem,
    nrecv_sem,
):
    me = lax.axis_index("dom")
    pool = lax.axis_index("pool")
    band = lax.axis_index("band")
    core = me % 2
    code_y = (me // 2) % 4
    code_x = me // 8

    def place_of(code):
        return code + (code // 2) * (1 - 2 * (code % 2))

    place_y = place_of(code_y)
    place_x = place_of(code_x)
    odd_y = place_y % 2
    odd_x = place_x % 2

    def in_copy(job):
        source = states if job < 4 else proj
        return pltpu.make_async_copy(
            source.at[pl.ds(16 * (job % 4), 16)], stage_in.at[job % 3], in_sem.at[job % 3]
        )

    for job in range(3):
        in_copy(job).start()

    barrier = pltpu.get_barrier_semaphore()
    for mask in ALL_MASKS:
        pl.semaphore_signal(
            barrier, inc=1, device_id={"dom": flip_bits(me, mask)}, device_id_type=MESH
        )
    mates = []
    for relation in range(1, 4):
        mate_pool = (pool + relation // 2) % 2
        mate_band = (band + relation % 2) % 2
        mates.append((mate_pool, mate_band))
        pl.semaphore_signal(
            barrier,
            inc=1,
            device_id={"pool": mate_pool, "band": mate_band},
            device_id_type=MESH,
        )

    def sign_of(direction, at_edge):
        sign = 1.0 - 2.0 * flips[0, direction].astype(F32)
        return jnp.where(at_edge, sign, jnp.float32(1.0))

    low_x, up_x = sign_of(0, place_x == 0), sign_of(0, place_x == 3)
    low_y, up_y = sign_of(1, place_y == 0), sign_of(1, place_y == 3)
    low_z, up_z = sign_of(2, core == 0), sign_of(2, core == 1)

    def halo_copies(phase, chunk):
        turn = CH * phase + chunk
        source = cur if phase == 0 else nxt
        plan = (
            (send_y.at[chunk, 1 - odd_y], recv_y.at[turn, 0], 2),
            (send_y.at[chunk, odd_y], recv_y.at[turn, 1], 4),
            (send_x.at[chunk, 1 - odd_x], recv_x.at[turn, 0], 8),
            (send_x.at[chunk, odd_x], recv_x.at[turn, 1], 16),
            (source.at[chunk], recv_z.at[turn], 1),
        )
        return [
            pltpu.make_async_remote_copy(
                src_ref=src,
                dst_ref=dst,
                send_sem=send_sem.at[turn, at],
                recv_sem=recv_sem.at[turn, at],
                device_id={"dom": flip_bits(me, mask)},
                device_id_type=MESH,
            )
            for at, (src, dst, mask) in enumerate(plan)
        ]

    lane8 = lax.broadcasted_iota(jnp.int32, (1, 8, 128), 2)

    def enqueue(phase, chunk):
        source = cur if phase == 0 else nxt
        copies = halo_copies(phase, chunk)
        copies[4].start()
        for face, first in ((0, 0), (1, CY - HALO)):
            value = jnp.concatenate(
                [source[chunk, pl.ds(x * CY + first, HALO)] for x in range(XL)], axis=0
            )
            tail = value[YROWS : YROWS + 3]
            for piece in range(15):
                send_y[chunk, face, 3 * piece : 3 * piece + 3] = jnp.where(
                    lane8 < USED, value[3 * piece : 3 * piece + 3], roll(tail, USED - 8 * piece)
                )
        copies[0].start()
        copies[1].start()
        for face, first in ((0, 0), (1, 2 * CY)):
            parts = [
                roll(
                    source[chunk, pl.ds(first + XROWS * group, XROWS)],
                    CZ * group - (GROUPS - 1) * CZ * face,
                )
                for group in range(GROUPS)
            ]
            send_x[chunk, face] = jnp.where(
                lane8 < CZ, parts[0], jnp.where(lane8 < 2 * CZ, parts[1], parts[2])
            )
        copies[2].start()
        copies[3].start()

    def stencil(phase, chunk):
        turn = CH * phase + chunk
        source, target = (cur, nxt) if phase == 0 else (nxt, cur)

        def z_part(half, carry):
            at = pl.ds(half * (ROWS // 2), ROWS // 2)
            left = jnp.concatenate(
                [
                    source[chunk, at].reshape(ROWS * 4, 128),
                    recv_z[turn, at].reshape(ROWS * 4, 128),
                ],
                axis=1,
            )
            high, rest = split(left)
            wide = jnp.dot(high, kz[...], preferred_element_type=F32)
            narrow = jnp.dot(rest, kz[:, :128], preferred_element_type=F32)
            total = (wide[:, :128] + wide[:, 128:] + narrow).reshape(ROWS // 2, 8, 128)
            if phase == 0:
                target[chunk, at] = total
            else:
                target[chunk, at] = total + total - target[chunk, at]
            return carry

        lax.fori_loop(0, 2, z_part, 0)

        for slot_of, sign, first in ((1 - odd_y, low_y, 0), (odd_y, up_y, HALO + CY)):
            rows = []
            tail = jnp.zeros((3, 8, 128), F32)
            for piece in range(15):
                value = recv_y[turn, slot_of, 3 * piece : 3 * piece + 3]
                rows.append(value)
                moved = roll(value, 8 * piece - USED)
                tail = jnp.where((lane8 >= 8 * piece) & (lane8 < 8 * piece + 8), moved, tail)
            rows = jnp.concatenate(rows + [tail], axis=0)
            rows = jnp.where(lane8 < USED, rows * sign, 0.0)
            for x in range(XL):
                ext_y[x, first : first + HALO] = rows[HALO * x : HALO * x + HALO]
        for x in range(XL):
            ext_y[x, HALO : HALO + CY] = source[chunk, x * CY : x * CY + CY]

        for group in range(GROUPS):
            lower = recv_x[turn, 1 - odd_x] * low_x
            ext_x[XROWS * group : XROWS * group + XROWS] = jnp.where(
                lane8 < CZ,
                roll(lower, -CZ * group),
                roll(source[chunk, pl.ds(2 * CY + XROWS * group, XROWS)], CZ),
            )
            upper = recv_x[turn, odd_x] * up_x
            start = (HALO + XL) * CY + XROWS * group
            ext_x[start : start + XROWS] = jnp.where(
                lane8 >= 2 * CZ,
                roll(upper, CZ * (GROUPS - 1 - group)),
                roll(source[chunk, pl.ds(XROWS * group, XROWS)], -CZ),
            )
        ext_x[HALO * CY : (HALO + XL) * CY] = source[chunk]

        def rest_part(step, carry):
            x, half = step // 2, step % 2
            at = pl.ds(x * CY + half * 10, 10)
            column = ext_y[x, pl.ds(half * 10, 10 + 2 * HALO)]
            total = potential[at] * column[HALO : HALO + 10]
            for shift in range(1, HALO + 1):
                pair = column[HALO + shift : HALO + shift + 10] + column[HALO - shift : HALO - shift + 10]
                above = ext_x[pl.ds((x + HALO + shift) * CY + half * 10, 10)]
                below = ext_x[pl.ds((x + HALO - shift) * CY + half * 10, 10)]
                total = total + (SCALE * COEFFS[shift]) * (pair + (above + below))
            if phase == 0:
                target[chunk, at] = target[chunk, at] + total
            else:
                target[chunk, at] = target[chunk, at] + (total + total)
            return carry

        lax.fori_loop(0, 2 * XL, rest_part, 0)

    own_slot = core * 16 + me // 2

    def gather_copies(phase, stage):
        buffer = gather1 if phase == 0 else gather2
        if stage == 0:
            masks, block = Y_MASKS, buffer.at[own_slot]
        elif stage == 1:
            masks, block = X_MASKS, buffer.at[pl.ds(core * 16 + code_x * 4, 4)]
        else:
            masks, block = (1,), buffer.at[pl.ds(core * 16, 16)]
        return [
            pltpu.make_async_remote_copy(
                src_ref=block,
                dst_ref=block,
                send_sem=gsend_sem.at[phase, 3 * stage + at],
                recv_sem=grecv_sem.at[phase, 3 * stage + at],
                device_id={"dom": flip_bits(me, mask)},
                device_id_type=MESH,
            )
            for at, mask in enumerate(masks)
        ]

    def gather_start(phase, stage):
        for copy in gather_copies(phase, stage):
            copy.start()

    def gather_wait(phase, stage):
        for copy in gather_copies(phase, stage):
            copy.wait()

    lane32 = lanes_of(32)

    def coefficients(phase):
        source = cur if phase == 0 else nxt
        buffer = gather1 if phase == 0 else gather2

        def step(pair, total):
            left = jnp.concatenate(
                [source[:, 2 * pair + part].reshape(STATES, 128) for part in range(2)], axis=1
            )
            both = jnp.concatenate(split(left), axis=0)
            return total + lax.dot_general(
                both, pbox[pair], (((1,), (1,)), ((), ())), preferred_element_type=F32
            )

        total = lax.fori_loop(0, PAIRS, step, jnp.zeros((128, 128), F32), unroll=4)
        total = total + roll(total, 64)
        total = total[:STATES] + total[STATES:]
        buffer[own_slot, 0:32] = jnp.where(lane32 < 64, total[:32], total[32:])

    def nonlocal_rows(phase):
        buffer = gather1 if phase == 0 else gather2

        def step(slot, total):
            block = buffer[slot, 0:32]
            pieces = []
            for piece in split(block):
                wide = piece.astype(F32)
                pieces.append(jnp.where(lane32 < 64, wide, 0.0))
                pieces.append(jnp.where(lane32 < 64, 0.0, wide))
            left = jnp.concatenate(pieces, axis=0).astype(BF16)
            return total + lax.dot_general(
                left, same[slot], (((1,), (1,)), ((), ())), preferred_element_type=F32
            )

        total = lax.fori_loop(0, 32, step, jnp.zeros((128, 128), F32), unroll=4)
        weights = (total[:STATES] + total[STATES:]) * coupling_row
        weights = weights * ((phase + 1.0) / HALF_WIDTH)
        left = jnp.concatenate(split(weights), axis=1)

        def spread(pair, carry):
            right = jnp.concatenate([pbox[pair], pbox[pair]], axis=0)
            both = jnp.dot(left, right, preferred_element_type=F32)
            nonloc[:, 2 * pair] = both[:, :128].reshape(CH, 8, 128)
            nonloc[:, 2 * pair + 1] = both[:, 128:].reshape(CH, 8, 128)
            return carry

        lax.fori_loop(0, PAIRS, spread, 0, unroll=4)

    def bring_states(job):
        in_copy(job).wait()

        def block(index, carry):
            for half in range(2):

                def load(group, tile):
                    start = pl.multiple_of(THIRD * group + 640 * index + 128 * tile, 128)
                    return stage_in[job % 3, 8 * half : 8 * half + 8, pl.ds(start, 128)]

                def put(line, row):
                    cur[2 * job + half, LINES * index + line] = row

                rows_from_lines(load, 8, put)
            return carry

        lax.fori_loop(0, BLOCKS, block, 0)
        in_copy(job + 3).start()

    bring_states(0)
    pl.semaphore_wait(barrier, len(ALL_MASKS) + 3)
    enqueue(0, 0)
    enqueue(0, 1)
    bring_states(1)
    enqueue(0, 2)
    bring_states(2)
    bring_states(3)

    kz[0:128] = k_own[...]
    kz[128:256] = (k_low[...].astype(F32) * low_z + k_up[...].astype(F32) * up_z).astype(BF16)

    def potential_block(index, carry):
        def load(group, tile):
            start = pl.multiple_of(THIRD * group + 640 * index + 128 * tile, 128)
            return jnp.broadcast_to(pot[:, pl.ds(start, 128)], (8, 128))

        def put(line, row):
            potential[LINES * index + line] = (row - CENTER) / HALF_WIDTH + 3.0 * SCALE * COEFFS[0]

        rows_from_lines(load, 8, put)
        return carry

    lax.fori_loop(0, BLOCKS, potential_block, 0)

    def diagonal(size):
        return lax.broadcasted_iota(jnp.int32, (size, size), 0) == lax.broadcasted_iota(
            jnp.int32, (size, size), 1
        )

    id_row = ids[...].astype(F32)
    id_pair = jnp.concatenate([id_row, id_row], axis=1)
    id_column = jnp.sum(jnp.where(diagonal(128), id_pair, 0.0), axis=1, keepdims=True)
    all_ids = lax.broadcasted_iota(jnp.int32, (128, 512), 1).astype(F32)
    strength = jnp.sum(
        jnp.where(all_ids == id_column, coupling[...], 0.0), axis=1, keepdims=True
    )
    coupling_row = jnp.sum(jnp.where(diagonal(128), strength, 0.0), axis=0, keepdims=True)
    occ_column = jnp.sum(
        jnp.where(diagonal(STATES), occupation[...], 0.0), axis=1, keepdims=True
    )
    occ_rows[...] = jnp.broadcast_to(occ_column, (STATES, 128)).reshape(CH, 8, 128)
    square[...] = jnp.zeros((ROWS, 8, 128), F32)
    gather1[own_slot, 32:40] = jnp.broadcast_to(id_pair, (8, 128))

    for job in range(4, 8):
        in_copy(job).wait()

        def proj_block(index, carry):
            held = []

            def load(group, tile):
                start = pl.multiple_of(THIRD * group + 640 * index + 128 * tile, 128)
                return stage_in[job % 3, :, pl.ds(start, 128)]

            def put(line, row):
                held.append(row)
                if line % 2 == 1:
                    high, rest = split(jnp.concatenate(held[-2:], axis=1))
                    pair = (LINES // 2) * index + line // 2
                    pbox[pair, 16 * (job - 4) : 16 * (job - 4) + 16] = high
                    pbox[pair, 16 * job : 16 * job + 16] = rest

            rows_from_lines(load, 16, put)
            return carry

        lax.fori_loop(0, BLOCKS, proj_block, 0)
        if job + 3 < 8:
            in_copy(job + 3).start()

    coefficients(0)
    gather_start(0, 0)

    def phase_one(chunk, carry):
        for copy in halo_copies(0, chunk):
            copy.wait()

        @pl.when(chunk == 2)
        def _():
            gather_wait(0, 0)
            gather_start(0, 1)

        @pl.when(chunk == 3)
        def _():
            gather_wait(0, 1)
            gather_start(0, 2)

        @pl.when((chunk >= 1) & (chunk < 6))
        def _():
            enqueue(0, chunk + 2)

        @pl.when(chunk >= 6)
        def _():
            enqueue(1, chunk - 6)

        stencil(0, chunk)

        @pl.when(chunk == 4)
        def _():
            gather_wait(0, 2)

            def compare(slot, inner):
                same[slot] = jnp.where(id_column == gather1[slot, 32:33], 1.0, 0.0).astype(BF16)
                return inner

            lax.fori_loop(0, 32, compare, 0)
            nonlocal_rows(0)

        def finish(done, inner):
            nxt[done] = nxt[done] + nonloc[done]
            return inner

        low = jnp.where(chunk == 4, 0, chunk)
        high = jnp.where(chunk < 4, chunk, chunk + 1)
        lax.fori_loop(low, high, finish, 0)
        return carry

    lax.fori_loop(0, CH, phase_one, 0)

    coefficients(1)
    gather_start(1, 0)

    def out_copy(chunk):
        return pltpu.make_async_copy(
            stage_out.at[chunk % 2], out.at[pl.ds(8 * chunk, 8)], out_sem.at[chunk % 2]
        )

    def phase_two(chunk, carry):
        for copy in halo_copies(1, chunk):
            copy.wait()

        @pl.when(chunk == 1)
        def _():
            gather_wait(1, 0)
            gather_start(1, 1)

        @pl.when(chunk == 2)
        def _():
            gather_wait(1, 1)
            gather_start(1, 2)

        @pl.when(chunk < 6)
        def _():
            enqueue(1, chunk + 2)

        stencil(1, chunk)

        @pl.when(chunk == 3)
        def _():
            gather_wait(1, 2)
            nonlocal_rows(1)

        def finish(done, inner):
            @pl.when(done >= 2)
            def _():
                out_copy(done - 2).wait()

            weight = occ_rows[done]

            def block(index, deep):
                at = pl.ds(LINES * index, LINES)
                value = cur[done, at] + nonloc[done, at]
                square[at] = square[at] + value * value * weight

                def put(group, tile, found):
                    start = pl.multiple_of(THIRD * group + 640 * index + 128 * tile, 128)
                    stage_out[done % 2, :, pl.ds(start, 128)] = found

                lines_from_rows([value[line] for line in range(LINES)], put)
                return deep

            lax.fori_loop(0, BLOCKS, block, 0)
            out_copy(done).start()
            return inner

        low = jnp.where(chunk == 3, 0, chunk)
        high = jnp.where(chunk < 3, chunk, chunk + 1)
        lax.fori_loop(low, high, finish, 0)
        return carry

    lax.fori_loop(0, CH, phase_two, 0)

    own_numer = numer[0].astype(F32)

    def rho_block(index, carry):
        value = square[pl.ds(LINES * index, LINES)]

        def put(group, tile, found):
            start = pl.multiple_of(THIRD * group + 640 * index + 128 * tile, 128)
            rho[:, pl.ds(start, 128)] = jnp.sum(found, axis=0, keepdims=True) * own_numer

        lines_from_rows([value[line] for line in range(LINES)], put)
        return carry

    lax.fori_loop(0, BLOCKS, rho_block, 0)
    for quarter in range(4):
        start = 128 * (75 * quarter // 2)
        notes[quarter, :, 0:PIECE] = rho[:, start : start + PIECE]
        notes[quarter, :, PIECE:NOTE] = jnp.full((1, 128), own_numer, F32)
    note_copies = [
        pltpu.make_async_remote_copy(
            src_ref=notes.at[2 * mate_pool + mate_band],
            dst_ref=got_notes.at[at],
            send_sem=nsend_sem.at[at],
            recv_sem=nrecv_sem.at[at],
            device_id={"pool": mate_pool, "band": mate_band},
            device_id_type=MESH,
        )
        for at, (mate_pool, mate_band) in enumerate(mates)
    ]
    for copy in note_copies:
        copy.start()
    for copy in note_copies:
        copy.wait()
    total = notes[2 * pool + band] + got_notes[0] + got_notes[1] + got_notes[2]
    count = total[:, PIECE : PIECE + 1] * 0.5
    dens[...] = total[:, :PIECE] / count
    for chunk in range(CH - 2, CH):
        out_copy(chunk).wait()


def body(
    states_in, bloch_flip, kweight_num, local_pot, proj_values, proj_ids, coupling, occupation
):
    k_own, k_low, k_up = z_matrices()
    vmem = pl.BlockSpec(memory_space=pltpu.VMEM)
    smem = pl.BlockSpec(memory_space=pltpu.SMEM)
    hbm = pl.BlockSpec(memory_space=pl.ANY)
    dma = pltpu.SemaphoreType.DMA
    out, dens = pl.pallas_call(
        kernel,
        out_shape=(
            jax.ShapeDtypeStruct((STATES, CELLS), F32),
            jax.ShapeDtypeStruct((1, PIECE), F32),
        ),
        in_specs=[hbm, smem, smem, vmem, hbm, vmem, vmem, vmem, vmem, vmem, vmem],
        out_specs=(hbm, vmem),
        scratch_shapes=[
            pltpu.VMEM((CH, ROWS, 8, 128), F32),
            pltpu.VMEM((CH, ROWS, 8, 128), F32),
            pltpu.VMEM((CH, ROWS, 8, 128), F32),
            pltpu.VMEM((PAIRS, 2 * SLOTS, 256), BF16),
            pltpu.VMEM((CH, 2, YROWS, 8, 128), F32),
            pltpu.VMEM((CH, 2, XROWS, 8, 128), F32),
            pltpu.VMEM((2 * CH, 2, YROWS, 8, 128), F32),
            pltpu.VMEM((2 * CH, 2, XROWS, 8, 128), F32),
            pltpu.VMEM((2 * CH, ROWS, 8, 128), F32),
            pltpu.VMEM(((XL + 2 * HALO) * CY, 8, 128), F32),
            pltpu.VMEM((XL, CY + 2 * HALO, 8, 128), F32),
            pltpu.VMEM((ROWS, 8, 128), F32),
            pltpu.VMEM((256, 256), BF16),
            pltpu.VMEM((32, 40, 128), F32),
            pltpu.VMEM((32, 32, 128), F32),
            pltpu.VMEM((32, 128, 128), BF16),
            pltpu.VMEM((CH, 8, 128), F32),
            pltpu.VMEM((ROWS, 8, 128), F32),
            pltpu.VMEM((1, CELLS), F32),
            pltpu.VMEM((4, 1, NOTE), F32),
            pltpu.VMEM((3, 1, NOTE), F32),
            pltpu.VMEM((3, 16, CELLS), F32),
            pltpu.VMEM((2, 8, CELLS), F32),
            dma((3,)),
            dma((2,)),
            dma((2 * CH, 5)),
            dma((2 * CH, 5)),
            dma((2, 9)),
            dma((2, 9)),
            dma((3,)),
            dma((3,)),
        ],
        compiler_params=pltpu.CompilerParams(
            collective_id=0, has_side_effects=True, vmem_limit_bytes=62 << 20
        ),
    )(
        states_in[0, 0],
        bloch_flip,
        kweight_num,
        local_pot,
        proj_values[0],
        proj_ids,
        coupling[None],
        occupation[None],
        k_own,
        k_low,
        k_up,
    )
    offset = 64 * lax.axis_index("band")
    quarter = lax.dynamic_slice(dens, (0, offset), (1, CELLS // 4))
    return out[None, None], quarter


def solution(mesh):
    placed = (
        P("pool", "dom", "band", None),
        P("pool", None),
        P("pool"),
        P("dom", None),
        P("dom", None, None),
        P("dom", None),
        P(),
        P("band"),
    )
    return jax.shard_map(
        body,
        mesh=mesh,
        in_specs=placed,
        out_specs=(P("pool", "dom", "band", None), P("dom", ("pool", "band"))),
        check_vma=False,
    )
```

time: 826 us -> 157 us (0.19); the launches traced: 817 us -> 157 us
  matrix products: 343 us -> 0 us
  waiting for transfers between devices: 331 us -> 0 us
  Pallas kernels: 0 us -> 149 us
  other arithmetic: 51.5 us -> 0 us
  local copies, waits for them, and re-layouts: 48.8 us -> 6.41 us
  between operations: 18.8 us -> 1.29 us
  starting transfers between devices: 17.2 us -> 0 us
    dot_general x8 -> x0, matrix products: 343 us -> none  [the longest x2 319 us: hamilton(): jnp.dot(back, proj_flat, precision=highest).reshape(field.shape)]
    psum x2 -> x0, waiting for transfers between devices: 256 us -> none  [hamilton(): total = lax.psum(partial_sums, 'dom')]
    pallas_call x0 -> x1, Pallas kernels: none -> 149 us  [body(): pl.pallas_call(kernel, out_shape=(jax.ShapeDtypeStruct((STATES, CELLS), F...]
    unnamed x4 -> x0, waiting for transfers between devices: 74.6 us -> none
    mul x9 -> x0, other arithmetic: 26.8 us -> none  [the longest x4 20.1 us: faces_of(): jnp.where(even, got_low, got_high) * jnp.where(place == 3, sign, 1.0)]
    unnamed x30 -> x1, local copies, waits for them, and re-layouts: 29.4 us -> 4.96 us
    select_n x4 -> x0, other arithmetic: 21.8 us -> none  [faces_of(): got_low = neighbour(jnp.where(even, top, bottom), first_bit)]
    ppermute x10 -> x0, starting transfers between devices: 16.6 us -> none  [partner(): return lax.ppermute(value, axis, pairs)]
  transfers between devices with their start and end apart: 13 -> 0, of which waited for: 3 -> 0; matrix products, arithmetic and copies ran while one was open for 10% -> 0% of each run, Pallas kernels for 0% -> 0%
where the time goes in v1:
time: 157 us
  Pallas kernels  149 us (95%)
  local copies, waits for them, and re-layouts  6.41 us (4%)
    pallas_call x1, Pallas kernels, body(): pl.pallas_call(kernel, out_shape=(jax.ShapeDtypeStruct((STATES, CELLS), F...  149 us
    unnamed x1, local copies, waits for them, and re-layouts  4.96 us

profile of v1, /device:TPU:0, one launch (start us, length us, event | category | flops | bytes accessed | tf_op | source)
XLA Modules:
  0.0 156.9 jit_solution(18303277341190898159)
XLA Ops:
  1.3 149.2 %shard_map.149 = (f32[64,19200]{1,0:T(8,128)}, f32[1,4864]{1,0:T(1,128)}) custom-call(f32[64,19200]{1,0:T(8,128)} %bitcast.5, s32[1,3]{1,0:T(1,128)} %flips.1, s32[1]{0:T(128)S(6)} %copy.17.numer, f32[1,19200]{1,0:T(1,128)} %pot.1, f32[64,19200]{1,0:T(8,128)} %bitcast.6, s32[1,64]{1,0:T(1,128)} %ids.1, f32[1,512]{1,0:T(1,128)} %bitcast.8, f32[1,64]{1,0:T(1,128)} %bitcast.9, ...), custom_call_target="tpu_custom_call" | custom-call | tf_op jit(solution)/shard_map/pallas_call | solution.py:670
  150.5 1.4 constant_dynamic-slice_fusion
  152.0 5.0 %copy.18 = f32[1,1,64,19200]{3,2,1,0:T(8,128)} copy(f32[1,1,64,19200]{3,2,1,0:T(8,128)} %bitcast.7) | data formatting | bytes 9830400

commit v2 on v1

--- a/solution.py
+++ b/solution.py
@@ -154,9 +154,7 @@
     notes,
     got_notes,
     stage_in,
-    stage_out,
     in_sem,
-    out_sem,
     send_sem,
     recv_sem,
     gsend_sem,
@@ -560,11 +558,6 @@
     coefficients(1)
     gather_start(1, 0)
 
-    def out_copy(chunk):
-        return pltpu.make_async_copy(
-            stage_out.at[chunk % 2], out.at[pl.ds(8 * chunk, 8)], out_sem.at[chunk % 2]
-        )
-
     def phase_two(chunk, carry):
         for copy in halo_copies(1, chunk):
             copy.wait()
@@ -591,10 +584,6 @@
             nonlocal_rows(1)
 
         def finish(done, inner):
-            @pl.when(done >= 2)
-            def _():
-                out_copy(done - 2).wait()
-
             weight = occ_rows[done]
 
             def block(index, deep):
@@ -604,13 +593,12 @@
 
                 def put(group, tile, found):
                     start = pl.multiple_of(THIRD * group + 640 * index + 128 * tile, 128)
-                    stage_out[done % 2, :, pl.ds(start, 128)] = found
+                    out[pl.ds(pl.multiple_of(8 * done, 8), 8), pl.ds(start, 128)] = found
 
                 lines_from_rows([value[line] for line in range(LINES)], put)
                 return deep
 
             lax.fori_loop(0, BLOCKS, block, 0)
-            out_copy(done).start()
             return inner
 
         low = jnp.where(chunk == 3, 0, chunk)
@@ -654,9 +642,8 @@
         copy.wait()
     total = notes[2 * pool + band] + got_notes[0] + got_notes[1] + got_notes[2]
     count = total[:, PIECE : PIECE + 1] * 0.5
-    dens[...] = total[:, :PIECE] / count
-    for chunk in range(CH - 2, CH):
-        out_copy(chunk).wait()
+    total = jnp.where(band == 1, total[:, 64:PIECE], total[:, : PIECE - 64])
+    dens[...] = total / count
 
 
 def body(
@@ -670,11 +657,11 @@
     out, dens = pl.pallas_call(
         kernel,
         out_shape=(
-            jax.ShapeDtypeStruct((STATES, CELLS), F32),
-            jax.ShapeDtypeStruct((1, PIECE), F32),
+            pltpu.VMEM((STATES, CELLS), F32),
+            jax.ShapeDtypeStruct((1, CELLS // 4), F32),
         ),
         in_specs=[hbm, smem, smem, vmem, hbm, vmem, vmem, vmem, vmem, vmem, vmem],
-        out_specs=(hbm, vmem),
+        out_specs=(vmem, vmem),
         scratch_shapes=[
             pltpu.VMEM((CH, ROWS, 8, 128), F32),
             pltpu.VMEM((CH, ROWS, 8, 128), F32),
@@ -698,9 +685,7 @@
             pltpu.VMEM((4, 1, NOTE), F32),
             pltpu.VMEM((3, 1, NOTE), F32),
             pltpu.VMEM((3, 16, CELLS), F32),
-            pltpu.VMEM((2, 8, CELLS), F32),
             dma((3,)),
-            dma((2,)),
             dma((2 * CH, 5)),
             dma((2 * CH, 5)),
             dma((2, 9)),
@@ -709,7 +694,7 @@
             dma((3,)),
         ],
         compiler_params=pltpu.CompilerParams(
-            collective_id=0, has_side_effects=True, vmem_limit_bytes=62 << 20
+            collective_id=0, has_side_effects=True, vmem_limit_bytes=58 << 20
         ),
     )(
         states_in[0, 0],
@@ -724,9 +709,7 @@
         k_low,
         k_up,
     )
-    offset = 64 * lax.axis_index("band")
-    quarter = lax.dynamic_slice(dens, (0, offset), (1, CELLS // 4))
-    return out[None, None], quarter
+    return out[None, None], dens
 
 
 def solution(mesh):

time: 157 us -> 154 us (0.981)
  local copies, waits for them, and re-layouts: 6.41 us -> 2.86 us
    unnamed x1 -> x4, local copies, waits for them, and re-layouts: 4.96 us -> 2.86 us
where the time goes in v2:
time: 154 us; the launch traced here: 153 us
  Pallas kernels  149 us (97%)
  local copies, waits for them, and re-layouts  2.86 us (2%)
    pallas_call x1, Pallas kernels, body(): pl.pallas_call(kernel, out_shape=(pltpu.VMEM((STATES, CELLS), F32), jax.S...  149 us

profile of v2, /device:TPU:0, one launch (start us, length us, event | category | flops | bytes accessed | tf_op | source)
XLA Modules:
  0.0 153.4 jit_solution(15034294140309221484)
XLA Ops:
  1.3 149.3 %shard_map.149 = (f32[64,19200]{1,0:T(8,128)S(1)}, f32[1,4800]{1,0:T(1,128)}) custom-call(f32[64,19200]{1,0:T(8,128)} %bitcast.6, s32[1,3]{1,0:T(1,128)} %flips.1, s32[1]{0:T(128)S(6)} %copy.19.numer, f32[1,19200]{1,0:T(1,128)} %pot.1, f32[64,19200]{1,0:T(8,128)} %bitcast.7, s32[1,64]{1,0:T(1,128)} %ids.1, f32[1,512]{1,0:T(1,128)} %bitcast.8, ...), custom_call_target="tpu_custom_call" | custom-call | tf_op jit(solution)/shard_map/pallas_call | solution.py:657
  150.6 0.0 copy-start
  150.6 2.3 %copy.18 = f32[1,1,64,19200]{3,2,1,0:T(8,128)} copy(f32[1,1,64,19200]{3,2,1,0:T(8,128)S(1)} %bitcast.5) | data formatting | bytes 9830400
  152.8 0.0 copy-done
  152.8 0.6 copy.20
Async XLA Ops:
  150.6 2.3 %copy-start = (f32[1,4800]{1,0:T(1,128)S(1)}, f32[1,4800]{1,0:T(1,128)}, u32[]{:S(2)}) copy-start(f32[1,4800]{1,0:T(1,128)} %get-tuple-element.11) | copy-start | bytes 57604

commit v3 on v2

--- a/solution.py
+++ b/solution.py
@@ -42,7 +42,6 @@
 YROWS = 45
 XROWS = 40
 PIECE = 4864
-NOTE = PIECE + 128
 
 Y_MASKS = (2, 4, 6)
 X_MASKS = (8, 16, 24)
@@ -143,15 +142,15 @@
     recv_z,
     ext_x,
     ext_y,
+    halo_y,
     potential,
     kz,
     gather1,
     gather2,
     same,
     occ_rows,
-    square,
     rho,
-    notes,
+    count_note,
     got_notes,
     stage_in,
     in_sem,
@@ -177,14 +176,22 @@
     odd_y = place_y % 2
     odd_x = place_x % 2
 
-    def in_copy(job):
-        source = states if job < 4 else proj
+    def state_copy(chunk):
+        slot, half = (chunk // 2) % 3, chunk % 2
         return pltpu.make_async_copy(
-            source.at[pl.ds(16 * (job % 4), 16)], stage_in.at[job % 3], in_sem.at[job % 3]
+            states.at[pl.ds(8 * chunk, 8)],
+            stage_in.at[slot, pl.ds(8 * half, 8)],
+            in_sem.at[slot, half],
         )
 
-    for job in range(3):
-        in_copy(job).start()
+    def proj_copy(job):
+        slot = (job + 1) % 3
+        return pltpu.make_async_copy(
+            proj.at[pl.ds(16 * job, 16)], stage_in.at[slot], in_sem.at[slot, 0]
+        )
+
+    for chunk in range(6):
+        state_copy(chunk).start()
 
     barrier = pltpu.get_barrier_semaphore()
     for mask in ALL_MASKS:
@@ -211,7 +218,7 @@
     low_y, up_y = sign_of(1, place_y == 0), sign_of(1, place_y == 3)
     low_z, up_z = sign_of(2, core == 0), sign_of(2, core == 1)
 
-    def halo_copies(phase, chunk):
+    def halo_copies(phase, chunk, wanted):
         turn = CH * phase + chunk
         source = cur if phase == 0 else nxt
         plan = (
@@ -231,13 +238,14 @@
                 device_id_type=MESH,
             )
             for at, (src, dst, mask) in enumerate(plan)
+            if at in wanted
         ]
 
     lane8 = lax.broadcasted_iota(jnp.int32, (1, 8, 128), 2)
 
     def enqueue(phase, chunk):
         source = cur if phase == 0 else nxt
-        copies = halo_copies(phase, chunk)
+        copies = halo_copies(phase, chunk, range(5))
         copies[4].start()
         for face, first in ((0, 0), (1, CY - HALO)):
             value = jnp.concatenate(
@@ -264,7 +272,7 @@
         copies[2].start()
         copies[3].start()
 
-    def stencil(phase, chunk):
+    def inner_part(phase, chunk):
         turn = CH * phase + chunk
         source, target = (cur, nxt) if phase == 0 else (nxt, cur)
 
@@ -289,18 +297,6 @@
 
         lax.fori_loop(0, 2, z_part, 0)
 
-        for slot_of, sign, first in ((1 - odd_y, low_y, 0), (odd_y, up_y, HALO + CY)):
-            rows = []
-            tail = jnp.zeros((3, 8, 128), F32)
-            for piece in range(15):
-                value = recv_y[turn, slot_of, 3 * piece : 3 * piece + 3]
-                rows.append(value)
-                moved = roll(value, 8 * piece - USED)
-                tail = jnp.where((lane8 >= 8 * piece) & (lane8 < 8 * piece + 8), moved, tail)
-            rows = jnp.concatenate(rows + [tail], axis=0)
-            rows = jnp.where(lane8 < USED, rows * sign, 0.0)
-            for x in range(XL):
-                ext_y[x, first : first + HALO] = rows[HALO * x : HALO * x + HALO]
         for x in range(XL):
             ext_y[x, HALO : HALO + CY] = source[chunk, x * CY : x * CY + CY]
 
@@ -337,6 +333,44 @@
             return carry
 
         lax.fori_loop(0, 2 * XL, rest_part, 0)
+
+    def y_halo_part(phase, chunk):
+        turn = CH * phase + chunk
+        target = nxt if phase == 0 else cur
+        scale = SCALE * (phase + 1.0)
+        for face, slot_of, sign in ((0, 1 - odd_y, low_y), (1, odd_y, up_y)):
+            tail = jnp.zeros((3, 8, 128), F32)
+            for piece in range(15):
+                value = recv_y[turn, slot_of, 3 * piece : 3 * piece + 3]
+                halo_y[face, 3 * piece : 3 * piece + 3] = value * sign
+                moved = roll(value, 8 * piece - USED)
+                tail = jnp.where((lane8 >= 8 * piece) & (lane8 < 8 * piece + 8), moved, tail)
+            halo_y[face, YROWS : YROWS + 3] = tail * sign
+
+        def column(x, carry):
+            low = halo_y[0, pl.ds(HALO * x, HALO)]
+            up = halo_y[1, pl.ds(HALO * x, HALO)]
+            first, last = [], []
+            for y in range(HALO):
+                first.append(
+                    sum(
+                        (scale * COEFFS[shift]) * low[HALO + y - shift]
+                        for shift in range(y + 1, HALO + 1)
+                    )
+                )
+                last.append(
+                    sum(
+                        (scale * COEFFS[shift]) * up[y + shift - HALO]
+                        for shift in range(HALO - y, HALO + 1)
+                    )
+                )
+            at = pl.ds(x * CY, HALO)
+            target[chunk, at] = target[chunk, at] + jnp.stack(first)
+            at = pl.ds(x * CY + CY - HALO, HALO)
+            target[chunk, at] = target[chunk, at] + jnp.stack(last)
+            return carry
+
+        lax.fori_loop(0, XL, column, 0, unroll=2)
 
     own_slot = core * 16 + me // 2
 
@@ -417,34 +451,94 @@
 
         lax.fori_loop(0, PAIRS, spread, 0, unroll=4)
 
-    def bring_states(job):
-        in_copy(job).wait()
+    def bring_states(chunk):
+        state_copy(chunk).wait()
+        slot, half = (chunk // 2) % 3, chunk % 2
 
         def block(index, carry):
-            for half in range(2):
-
-                def load(group, tile):
-                    start = pl.multiple_of(THIRD * group + 640 * index + 128 * tile, 128)
-                    return stage_in[job % 3, 8 * half : 8 * half + 8, pl.ds(start, 128)]
-
-                def put(line, row):
-                    cur[2 * job + half, LINES * index + line] = row
-
-                rows_from_lines(load, 8, put)
+            def load(group, tile):
+                start = pl.multiple_of(THIRD * group + 640 * index + 128 * tile, 128)
+                return stage_in[slot, 8 * half : 8 * half + 8, pl.ds(start, 128)]
+
+            def put(line, row):
+                cur[chunk, LINES * index + line] = row
+
+            rows_from_lines(load, 8, put)
             return carry
 
-        lax.fori_loop(0, BLOCKS, block, 0)
-        in_copy(job + 3).start()
+        lax.fori_loop(0, BLOCKS, block, 0, unroll=5)
 
     bring_states(0)
     pl.semaphore_wait(barrier, len(ALL_MASKS) + 3)
     enqueue(0, 0)
+    bring_states(1)
     enqueue(0, 1)
-    bring_states(1)
+    state_copy(6).start()
+    state_copy(7).start()
+    bring_states(2)
     enqueue(0, 2)
-    bring_states(2)
+    own_numer = numer[0].astype(F32)
+    count_note[0] = jnp.full((1, 128), own_numer, F32)
+    count_copy = pltpu.make_async_remote_copy(
+        src_ref=count_note.at[0],
+        dst_ref=count_note.at[1],
+        send_sem=nsend_sem.at[3],
+        recv_sem=nrecv_sem.at[3],
+        device_id={"pool": (pool + 1) % 2, "band": band},
+        device_id_type=MESH,
+    )
+    count_copy.start()
     bring_states(3)
-
+    proj_copy(0).start()
+    bring_states(4)
+    bring_states(5)
+    proj_copy(1).start()
+    bring_states(6)
+    bring_states(7)
+    proj_copy(2).start()
+
+    def diagonal(size):
+        return lax.broadcasted_iota(jnp.int32, (size, size), 0) == lax.broadcasted_iota(
+            jnp.int32, (size, size), 1
+        )
+
+    id_row = ids[...].astype(F32)
+    id_pair = jnp.concatenate([id_row, id_row], axis=1)
+    id_column = jnp.sum(jnp.where(diagonal(128), id_pair, 0.0), axis=1, keepdims=True)
+    gather1[own_slot, 32:40] = jnp.broadcast_to(id_pair, (8, 128))
+
+    for job in range(4):
+        proj_copy(job).wait()
+
+        def proj_block(index, carry):
+            held = []
+
+            def load(group, tile):
+                start = pl.multiple_of(THIRD * group + 640 * index + 128 * tile, 128)
+                return stage_in[(job + 1) % 3, :, pl.ds(start, 128)]
+
+            def put(line, row):
+                held.append(row)
+                if line % 2 == 1:
+                    high, rest = split(jnp.concatenate(held[-2:], axis=1))
+                    pair = (LINES // 2) * index + line // 2
+                    pbox[pair, 16 * job : 16 * job + 16] = high
+                    pbox[pair, SLOTS + 16 * job : SLOTS + 16 * job + 16] = rest
+
+            rows_from_lines(load, 16, put)
+            return carry
+
+        lax.fori_loop(0, BLOCKS, proj_block, 0, unroll=5)
+        if job == 0:
+            proj_copy(3).start()
+
+    coefficients(0)
+    gather_start(0, 0)
+    enqueue(0, 3)
+
+    for x in range(XL):
+        ext_y[x, 0:HALO] = jnp.zeros((HALO, 8, 128), F32)
+        ext_y[x, HALO + CY :] = jnp.zeros((HALO, 8, 128), F32)
     kz[0:128] = k_own[...]
     kz[128:256] = (k_low[...].astype(F32) * low_z + k_up[...].astype(F32) * up_z).astype(BF16)
 
@@ -459,16 +553,8 @@
         rows_from_lines(load, 8, put)
         return carry
 
-    lax.fori_loop(0, BLOCKS, potential_block, 0)
-
-    def diagonal(size):
-        return lax.broadcasted_iota(jnp.int32, (size, size), 0) == lax.broadcasted_iota(
-            jnp.int32, (size, size), 1
-        )
-
-    id_row = ids[...].astype(F32)
-    id_pair = jnp.concatenate([id_row, id_row], axis=1)
-    id_column = jnp.sum(jnp.where(diagonal(128), id_pair, 0.0), axis=1, keepdims=True)
+    lax.fori_loop(0, BLOCKS, potential_block, 0, unroll=5)
+
     all_ids = lax.broadcasted_iota(jnp.int32, (128, 512), 1).astype(F32)
     strength = jnp.sum(
         jnp.where(all_ids == id_column, coupling[...], 0.0), axis=1, keepdims=True
@@ -477,41 +563,19 @@
     occ_column = jnp.sum(
         jnp.where(diagonal(STATES), occupation[...], 0.0), axis=1, keepdims=True
     )
-    occ_rows[...] = jnp.broadcast_to(occ_column, (STATES, 128)).reshape(CH, 8, 128)
-    square[...] = jnp.zeros((ROWS, 8, 128), F32)
-    gather1[own_slot, 32:40] = jnp.broadcast_to(id_pair, (8, 128))
-
-    for job in range(4, 8):
-        in_copy(job).wait()
-
-        def proj_block(index, carry):
-            held = []
-
-            def load(group, tile):
-                start = pl.multiple_of(THIRD * group + 640 * index + 128 * tile, 128)
-                return stage_in[job % 3, :, pl.ds(start, 128)]
-
-            def put(line, row):
-                held.append(row)
-                if line % 2 == 1:
-                    high, rest = split(jnp.concatenate(held[-2:], axis=1))
-                    pair = (LINES // 2) * index + line // 2
-                    pbox[pair, 16 * (job - 4) : 16 * (job - 4) + 16] = high
-                    pbox[pair, 16 * job : 16 * job + 16] = rest
-
-            rows_from_lines(load, 16, put)
-            return carry
-
-        lax.fori_loop(0, BLOCKS, proj_block, 0)
-        if job + 3 < 8:
-            in_copy(job + 3).start()
-
-    coefficients(0)
-    gather_start(0, 0)
+    occ_rows[...] = jnp.broadcast_to(occ_column * own_numer, (STATES, 128)).reshape(CH, 8, 128)
+    rho[...] = jnp.zeros((1, CELLS), F32)
+
+    def wait_y(phase, chunk):
+        for copy in halo_copies(phase, chunk, (0, 1)):
+            copy.wait()
+
+    def wait_rest(phase, chunk):
+        for copy in halo_copies(phase, chunk, (2, 3, 4)):
+            copy.wait()
 
     def phase_one(chunk, carry):
-        for copy in halo_copies(0, chunk):
-            copy.wait()
+        wait_y(0, chunk)
 
         @pl.when(chunk == 2)
         def _():
@@ -523,7 +587,7 @@
             gather_wait(0, 1)
             gather_start(0, 2)
 
-        @pl.when((chunk >= 1) & (chunk < 6))
+        @pl.when((chunk >= 2) & (chunk < 6))
         def _():
             enqueue(0, chunk + 2)
 
@@ -531,7 +595,7 @@
         def _():
             enqueue(1, chunk - 6)
 
-        stencil(0, chunk)
+        y_halo_part(0, chunk)
 
         @pl.when(chunk == 4)
         def _():
@@ -551,16 +615,23 @@
         low = jnp.where(chunk == 4, 0, chunk)
         high = jnp.where(chunk < 4, chunk, chunk + 1)
         lax.fori_loop(low, high, finish, 0)
+
+        @pl.when(chunk < CH - 1)
+        def _():
+            wait_rest(0, chunk + 1)
+            inner_part(0, chunk + 1)
+
         return carry
 
+    wait_rest(0, 0)
+    inner_part(0, 0)
     lax.fori_loop(0, CH, phase_one, 0)
 
     coefficients(1)
     gather_start(1, 0)
 
     def phase_two(chunk, carry):
-        for copy in halo_copies(1, chunk):
-            copy.wait()
+        wait_y(1, chunk)
 
         @pl.when(chunk == 1)
         def _():
@@ -576,7 +647,7 @@
         def _():
             enqueue(1, chunk + 2)
 
-        stencil(1, chunk)
+        y_halo_part(1, chunk)
 
         @pl.when(chunk == 3)
         def _():
@@ -589,45 +660,41 @@
             def block(index, deep):
                 at = pl.ds(LINES * index, LINES)
                 value = cur[done, at] + nonloc[done, at]
-                square[at] = square[at] + value * value * weight
-
                 def put(group, tile, found):
                     start = pl.multiple_of(THIRD * group + 640 * index + 128 * tile, 128)
                     out[pl.ds(pl.multiple_of(8 * done, 8), 8), pl.ds(start, 128)] = found
+                    rho[:, pl.ds(start, 128)] = rho[:, pl.ds(start, 128)] + jnp.sum(
+                        found * found * weight, axis=0, keepdims=True
+                    )
 
                 lines_from_rows([value[line] for line in range(LINES)], put)
                 return deep
 
-            lax.fori_loop(0, BLOCKS, block, 0)
+            lax.fori_loop(0, BLOCKS, block, 0, unroll=5)
             return inner
 
         low = jnp.where(chunk == 3, 0, chunk)
         high = jnp.where(chunk < 3, chunk, chunk + 1)
         lax.fori_loop(low, high, finish, 0)
+
+        @pl.when(chunk < CH - 1)
+        def _():
+            wait_rest(1, chunk + 1)
+            inner_part(1, chunk + 1)
+
         return carry
 
+    wait_rest(1, 0)
+    inner_part(1, 0)
     lax.fori_loop(0, CH, phase_two, 0)
 
-    own_numer = numer[0].astype(F32)
-
-    def rho_block(index, carry):
-        value = square[pl.ds(LINES * index, LINES)]
-
-        def put(group, tile, found):
-            start = pl.multiple_of(THIRD * group + 640 * index + 128 * tile, 128)
-            rho[:, pl.ds(start, 128)] = jnp.sum(found, axis=0, keepdims=True) * own_numer
-
-        lines_from_rows([value[line] for line in range(LINES)], put)
-        return carry
-
-    lax.fori_loop(0, BLOCKS, rho_block, 0)
-    for quarter in range(4):
-        start = 128 * (75 * quarter // 2)
-        notes[quarter, :, 0:PIECE] = rho[:, start : start + PIECE]
-        notes[quarter, :, PIECE:NOTE] = jnp.full((1, 128), own_numer, F32)
+    def quarter_of(mate_pool, mate_band):
+        start = pl.multiple_of(128 * (75 * (2 * mate_pool + mate_band) // 2), 128)
+        return pl.ds(start, PIECE)
+
     note_copies = [
         pltpu.make_async_remote_copy(
-            src_ref=notes.at[2 * mate_pool + mate_band],
+            src_ref=rho.at[:, quarter_of(mate_pool, mate_band)],
             dst_ref=got_notes.at[at],
             send_sem=nsend_sem.at[at],
             recv_sem=nrecv_sem.at[at],
@@ -636,14 +703,15 @@
         )
         for at, (mate_pool, mate_band) in enumerate(mates)
     ]
-    for copy in note_copies:
+    for copy in note_copies[::-1]:
         copy.start()
+    count_copy.wait()
+    total_numer = count_note[0] + count_note[1]
     for copy in note_copies:
         copy.wait()
-    total = notes[2 * pool + band] + got_notes[0] + got_notes[1] + got_notes[2]
-    count = total[:, PIECE : PIECE + 1] * 0.5
+    total = rho[:, quarter_of(pool, band)] + got_notes[0] + got_notes[1] + got_notes[2]
     total = jnp.where(band == 1, total[:, 64:PIECE], total[:, : PIECE - 64])
-    dens[...] = total / count
+    dens[...] = total / total_numer[:, 0:1]
 
 
 def body(
@@ -658,7 +726,7 @@
         kernel,
         out_shape=(
             pltpu.VMEM((STATES, CELLS), F32),
-            jax.ShapeDtypeStruct((1, CELLS // 4), F32),
+            pltpu.VMEM((1, CELLS // 4), F32),
         ),
         in_specs=[hbm, smem, smem, vmem, hbm, vmem, vmem, vmem, vmem, vmem, vmem],
         out_specs=(vmem, vmem),
@@ -674,24 +742,24 @@
             pltpu.VMEM((2 * CH, ROWS, 8, 128), F32),
             pltpu.VMEM(((XL + 2 * HALO) * CY, 8, 128), F32),
             pltpu.VMEM((XL, CY + 2 * HALO, 8, 128), F32),
+            pltpu.VMEM((2, XL * HALO, 8, 128), F32),
             pltpu.VMEM((ROWS, 8, 128), F32),
             pltpu.VMEM((256, 256), BF16),
             pltpu.VMEM((32, 40, 128), F32),
             pltpu.VMEM((32, 32, 128), F32),
             pltpu.VMEM((32, 128, 128), BF16),
             pltpu.VMEM((CH, 8, 128), F32),
-            pltpu.VMEM((ROWS, 8, 128), F32),
             pltpu.VMEM((1, CELLS), F32),
-            pltpu.VMEM((4, 1, NOTE), F32),
-            pltpu.VMEM((3, 1, NOTE), F32),
+            pltpu.VMEM((2, 1, 128), F32),
+            pltpu.VMEM((3, 1, PIECE), F32),
             pltpu.VMEM((3, 16, CELLS), F32),
-            dma((3,)),
+            dma((3, 2)),
             dma((2 * CH, 5)),
             dma((2 * CH, 5)),
             dma((2, 9)),
             dma((2, 9)),
-            dma((3,)),
-            dma((3,)),
+            dma((4,)),
+            dma((4,)),
         ],
         compiler_params=pltpu.CompilerParams(
             collective_id=0, has_side_effects=True, vmem_limit_bytes=58 << 20

time: 154 us -> 149 us (0.968)
  Pallas kernels: 149 us -> 145 us
    pallas_call x1, Pallas kernels: 149 us -> 145 us  [body(): pl.pallas_call(kernel, out_shape=(pltpu.VMEM((STATES, CELLS), F32), pltpu...]
where the time goes in v3:
time: 149 us
  Pallas kernels  145 us (97%)
  local copies, waits for them, and re-layouts  2.86 us (2%)
    pallas_call x1, Pallas kernels, body(): pl.pallas_call(kernel, out_shape=(pltpu.VMEM((STATES, CELLS), F32), pltpu...  145 us

profile of v3, /device:TPU:0, one launch (start us, length us, event | category | flops | bytes accessed | tf_op | source)
XLA Modules:
  0.0 149.2 jit_solution(6839459290201025463)
XLA Ops:
  1.3 145.0 %shard_map.149 = (f32[64,19200]{1,0:T(8,128)S(1)}, f32[1,4800]{1,0:T(1,128)S(1)}) custom-call(f32[64,19200]{1,0:T(8,128)} %bitcast.6, s32[1,3]{1,0:T(1,128)} %flips.1, s32[1]{0:T(128)S(6)} %copy.20.numer, f32[1,19200]{1,0:T(1,128)} %pot.1, f32[64,19200]{1,0:T(8,128)} %bitcast.7, s32[1,64]{1,0:T(1,128)} %ids.1, f32[1,512]{1,0:T(1,128)} %bitcast.8, ...), custom_call_target="tpu_custom_call" | custom-call | tf_op jit(solution)/shard_map/pallas_call | solution.py:725
  146.3 2.3 %copy.18 = f32[1,1,64,19200]{3,2,1,0:T(8,128)} copy(f32[1,1,64,19200]{3,2,1,0:T(8,128)S(1)} %bitcast.5) | data formatting | bytes 9830400
  148.5 0.6 copy.19

commit v4 on v3

--- a/solution.py
+++ b/solution.py
@@ -119,16 +119,16 @@
 
 def kernel(
     states,
-    flips,
-    numer,
-    pot,
+    flips_in,
+    numer_in,
+    pot_in,
     proj,
-    ids,
-    coupling,
-    occupation,
-    k_own,
-    k_low,
-    k_up,
+    ids_in,
+    coupling_in,
+    occupation_in,
+    k_own_in,
+    k_low_in,
+    k_up_in,
     out,
     dens,
     cur,
@@ -153,7 +153,17 @@
     count_note,
     got_notes,
     stage_in,
+    flips,
+    numer,
+    pot,
+    ids,
+    coupling,
+    occupation,
+    k_own,
+    k_low,
+    k_up,
     in_sem,
+    small_sem,
     send_sem,
     recv_sem,
     gsend_sem,
@@ -190,9 +200,7 @@
             proj.at[pl.ds(16 * job, 16)], stage_in.at[slot], in_sem.at[slot, 0]
         )
 
-    for chunk in range(6):
-        state_copy(chunk).start()
-
+    state_copy(0).start()
     barrier = pltpu.get_barrier_semaphore()
     for mask in ALL_MASKS:
         pl.semaphore_signal(
@@ -210,13 +218,26 @@
             device_id_type=MESH,
         )
 
-    def sign_of(direction, at_edge):
-        sign = 1.0 - 2.0 * flips[0, direction].astype(F32)
-        return jnp.where(at_edge, sign, jnp.float32(1.0))
-
-    low_x, up_x = sign_of(0, place_x == 0), sign_of(0, place_x == 3)
-    low_y, up_y = sign_of(1, place_y == 0), sign_of(1, place_y == 3)
-    low_z, up_z = sign_of(2, core == 0), sign_of(2, core == 1)
+    for chunk in range(1, 6):
+        state_copy(chunk).start()
+    small = [
+        pltpu.make_async_copy(source, held, small_sem.at[at])
+        for at, (source, held) in enumerate(
+            (
+                (flips_in, flips),
+                (numer_in, numer),
+                (pot_in, pot),
+                (ids_in, ids),
+                (coupling_in, coupling),
+                (occupation_in, occupation),
+                (k_own_in, k_own),
+                (k_low_in, k_low),
+                (k_up_in, k_up),
+            )
+        )
+    ]
+    for copy in small:
+        copy.start()
 
     def halo_copies(phase, chunk, wanted):
         turn = CH * phase + chunk
@@ -246,7 +267,6 @@
     def enqueue(phase, chunk):
         source = cur if phase == 0 else nxt
         copies = halo_copies(phase, chunk, range(5))
-        copies[4].start()
         for face, first in ((0, 0), (1, CY - HALO)):
             value = jnp.concatenate(
                 [source[chunk, pl.ds(x * CY + first, HALO)] for x in range(XL)], axis=0
@@ -258,6 +278,7 @@
                 )
         copies[0].start()
         copies[1].start()
+        copies[4].start()
         for face, first in ((0, 0), (1, 2 * CY)):
             parts = [
                 roll(
@@ -370,7 +391,7 @@
             target[chunk, at] = target[chunk, at] + jnp.stack(last)
             return carry
 
-        lax.fori_loop(0, XL, column, 0, unroll=2)
+        lax.fori_loop(0, XL, column, 0, unroll=4)
 
     own_slot = core * 16 + me // 2
 
@@ -477,8 +498,27 @@
     state_copy(7).start()
     bring_states(2)
     enqueue(0, 2)
-    own_numer = numer[0].astype(F32)
-    count_note[0] = jnp.full((1, 128), own_numer, F32)
+    bring_states(3)
+    proj_copy(0).start()
+    bring_states(4)
+    bring_states(5)
+    proj_copy(1).start()
+    bring_states(6)
+    bring_states(7)
+    proj_copy(2).start()
+
+    for copy in small:
+        copy.wait()
+    def sign_of(direction, at_edge):
+        flip = flips[:, direction : direction + 1].astype(F32) * at_edge.astype(F32)
+        return jnp.broadcast_to(1.0 - 2.0 * flip, (8, 128))
+
+    low_x, up_x = sign_of(0, place_x == 0), sign_of(0, place_x == 3)
+    low_y, up_y = sign_of(1, place_y == 0), sign_of(1, place_y == 3)
+    low_z, up_z = sign_of(2, core == 0), sign_of(2, core == 1)
+
+    own_numer = numer[...].astype(F32)
+    count_note[0] = jnp.broadcast_to(own_numer, (1, 128))
     count_copy = pltpu.make_async_remote_copy(
         src_ref=count_note.at[0],
         dst_ref=count_note.at[1],
@@ -488,15 +528,6 @@
         device_id_type=MESH,
     )
     count_copy.start()
-    bring_states(3)
-    proj_copy(0).start()
-    bring_states(4)
-    bring_states(5)
-    proj_copy(1).start()
-    bring_states(6)
-    bring_states(7)
-    proj_copy(2).start()
-
     def diagonal(size):
         return lax.broadcasted_iota(jnp.int32, (size, size), 0) == lax.broadcasted_iota(
             jnp.int32, (size, size), 1
@@ -540,7 +571,9 @@
         ext_y[x, 0:HALO] = jnp.zeros((HALO, 8, 128), F32)
         ext_y[x, HALO + CY :] = jnp.zeros((HALO, 8, 128), F32)
     kz[0:128] = k_own[...]
-    kz[128:256] = (k_low[...].astype(F32) * low_z + k_up[...].astype(F32) * up_z).astype(BF16)
+    kz[128:256] = (
+        k_low[...].astype(F32) * low_z[0:1, 0:1] + k_up[...].astype(F32) * up_z[0:1, 0:1]
+    ).astype(BF16)
 
     def potential_block(index, carry):
         def load(group, tile):
@@ -670,7 +703,7 @@
                 lines_from_rows([value[line] for line in range(LINES)], put)
                 return deep
 
-            lax.fori_loop(0, BLOCKS, block, 0, unroll=5)
+            lax.fori_loop(0, BLOCKS, block, 0, unroll=10)
             return inner
 
         low = jnp.where(chunk == 3, 0, chunk)
@@ -719,7 +752,6 @@
 ):
     k_own, k_low, k_up = z_matrices()
     vmem = pl.BlockSpec(memory_space=pltpu.VMEM)
-    smem = pl.BlockSpec(memory_space=pltpu.SMEM)
     hbm = pl.BlockSpec(memory_space=pl.ANY)
     dma = pltpu.SemaphoreType.DMA
     out, dens = pl.pallas_call(
@@ -728,7 +760,7 @@
             pltpu.VMEM((STATES, CELLS), F32),
             pltpu.VMEM((1, CELLS // 4), F32),
         ),
-        in_specs=[hbm, smem, smem, vmem, hbm, vmem, vmem, vmem, vmem, vmem, vmem],
+        in_specs=[hbm] * 11,
         out_specs=(vmem, vmem),
         scratch_shapes=[
             pltpu.VMEM((CH, ROWS, 8, 128), F32),
@@ -753,7 +785,17 @@
             pltpu.VMEM((2, 1, 128), F32),
             pltpu.VMEM((3, 1, PIECE), F32),
             pltpu.VMEM((3, 16, CELLS), F32),
+            pltpu.VMEM((1, 3), jnp.int32),
+            pltpu.VMEM((1, 1), jnp.int32),
+            pltpu.VMEM((1, CELLS), F32),
+            pltpu.VMEM((1, SLOTS), jnp.int32),
+            pltpu.VMEM((1, 512), F32),
+            pltpu.VMEM((1, STATES), F32),
+            pltpu.VMEM((128, 256), BF16),
+            pltpu.VMEM((128, 256), BF16),
+            pltpu.VMEM((128, 256), BF16),
             dma((3, 2)),
+            dma((9,)),
             dma((2 * CH, 5)),
             dma((2 * CH, 5)),
             dma((2, 9)),
@@ -767,7 +809,7 @@
     )(
         states_in[0, 0],
         bloch_flip,
-        kweight_num,
+        kweight_num[None],
         local_pot,
         proj_values[0],
         proj_ids,
@@ -776,6 +818,32 @@
         k_own,
         k_low,
         k_up,
+    )
+
+    def move(held, held_dens, result, result_dens, sem):
+        copies = [
+            pltpu.make_async_copy(held.at[pl.ds(8 * at, 8)], result.at[pl.ds(8 * at, 8)], sem.at[at])
+            for at in range(CH)
+        ]
+        copies.append(pltpu.make_async_copy(held_dens, result_dens, sem.at[CH]))
+        for copy in copies:
+            copy.start()
+        for copy in copies:
+            copy.wait()
+
+    out, dens = pl.pallas_call(
+        move,
+        out_shape=(
+            jax.ShapeDtypeStruct((STATES, CELLS), F32),
+            jax.ShapeDtypeStruct((1, CELLS // 4), F32),
+        ),
+        in_specs=[vmem, vmem],
+        out_specs=(hbm, hbm),
+        scratch_shapes=[dma((CH + 1,))],
+        compiler_params=pltpu.CompilerParams(vmem_limit_bytes=1 << 20),
+    )(
+        pltpu.with_memory_space_constraint(out, pltpu.VMEM),
+        pltpu.with_memory_space_constraint(dens, pltpu.VMEM),
     )
     return out[None, None], dens
 

time: 149 us -> 147 us (0.987)
  local copies, waits for them, and re-layouts: 2.86 us -> 0 us
    unnamed x2 -> x0, local copies, waits for them, and re-layouts: 2.86 us -> none
    pallas_call x0 -> x1, Pallas kernels: none -> 2.32 us  [body(): pl.pallas_call(move, out_shape=(jax.ShapeDtypeStruct((STATES, CELLS), F32...]
where the time goes in v4:
time: 147 us
  Pallas kernels  146 us (99%)
    pallas_call x1, Pallas kernels, body(): pl.pallas_call(kernel, out_shape=(pltpu.VMEM((STATES, CELLS), F32), pltpu...  144 us

profile of v4, /device:TPU:0, one launch (start us, length us, event | category | flops | bytes accessed | tf_op | source)
XLA Modules:
  0.0 147.3 jit_solution(11575160349994034659)
XLA Ops:
  1.3 143.7 %shard_map.149 = (f32[64,19200]{1,0:T(8,128)S(1)}, f32[1,4800]{1,0:T(1,128)S(1)}) custom-call(f32[64,19200]{1,0:T(8,128)} %bitcast.7, s32[1,3]{1,0:T(1,128)} %flips_in.1, s32[1,1]{1,0:T(1,128)} %bitcast.6.numer_in, f32[1,19200]{1,0:T(1,128)} %pot_in.1, f32[64,19200]{1,0:T(8,128)} %bitcast.8, s32[1,64]{1,0:T(1,128)} %ids_in.1, f32[1,512]{1,0:T(1,128)} %bitcast.9, ...), custom_call_target="tpu_custom_call" | custom-call | tf_op jit(solution)/shard_map/pallas_call | solution.py:757
  144.9 2.3 %shard_map.150 = (f32[64,19200]{1,0:T(8,128)}, f32[1,4800]{1,0:T(1,128)}) custom-call(f32[64,19200]{1,0:T(8,128)S(1)} %get-tuple-element.6.held, f32[1,4800]{1,0:T(1,128)S(1)} %get-tuple-element.7.held_dens), custom_call_target="tpu_custom_call" | custom-call | tf_op jit(solution)/shard_map/pallas_call | solution.py:834

commit v5 on v4

--- a/solution.py
+++ b/solution.py
@@ -398,8 +398,10 @@
     def gather_copies(phase, stage):
         buffer = gather1 if phase == 0 else gather2
         if stage == 0:
-            masks, block = Y_MASKS, buffer.at[own_slot]
+            masks, block = (2, 6), buffer.at[own_slot]
         elif stage == 1:
+            masks, block = (6,), buffer.at[core * 16 + flip_bits(me, 2) // 2]
+        elif stage == 2:
             masks, block = X_MASKS, buffer.at[pl.ds(core * 16 + code_x * 4, 4)]
         else:
             masks, block = (1,), buffer.at[pl.ds(core * 16, 16)]
@@ -620,6 +622,11 @@
             gather_wait(0, 1)
             gather_start(0, 2)
 
+        @pl.when(chunk == 4)
+        def _():
+            gather_wait(0, 2)
+            gather_start(0, 3)
+
         @pl.when((chunk >= 2) & (chunk < 6))
         def _():
             enqueue(0, chunk + 2)
@@ -630,9 +637,9 @@
 
         y_halo_part(0, chunk)
 
-        @pl.when(chunk == 4)
-        def _():
-            gather_wait(0, 2)
+        @pl.when(chunk == 5)
+        def _():
+            gather_wait(0, 3)
 
             def compare(slot, inner):
                 same[slot] = jnp.where(id_column == gather1[slot, 32:33], 1.0, 0.0).astype(BF16)
@@ -645,8 +652,8 @@
             nxt[done] = nxt[done] + nonloc[done]
             return inner
 
-        low = jnp.where(chunk == 4, 0, chunk)
-        high = jnp.where(chunk < 4, chunk, chunk + 1)
+        low = jnp.where(chunk == 5, 0, chunk)
+        high = jnp.where(chunk < 5, chunk, chunk + 1)
         lax.fori_loop(low, high, finish, 0)
 
         @pl.when(chunk < CH - 1)
@@ -676,15 +683,20 @@
             gather_wait(1, 1)
             gather_start(1, 2)
 
+        @pl.when(chunk == 3)
+        def _():
+            gather_wait(1, 2)
+            gather_start(1, 3)
+
         @pl.when(chunk < 6)
         def _():
             enqueue(1, chunk + 2)
 
         y_halo_part(1, chunk)
 
-        @pl.when(chunk == 3)
-        def _():
-            gather_wait(1, 2)
+        @pl.when(chunk == 4)
+        def _():
+            gather_wait(1, 3)
             nonlocal_rows(1)
 
         def finish(done, inner):
@@ -706,8 +718,8 @@
             lax.fori_loop(0, BLOCKS, block, 0, unroll=10)
             return inner
 
-        low = jnp.where(chunk == 3, 0, chunk)
-        high = jnp.where(chunk < 3, chunk, chunk + 1)
+        low = jnp.where(chunk == 4, 0, chunk)
+        high = jnp.where(chunk < 4, chunk, chunk + 1)
         lax.fori_loop(low, high, finish, 0)
 
         @pl.when(chunk < CH - 1)
@@ -736,8 +748,8 @@
         )
         for at, (mate_pool, mate_band) in enumerate(mates)
     ]
-    for copy in note_copies[::-1]:
-        copy.start()
+    for at in (1, 2, 0):
+        note_copies[at].start()
     count_copy.wait()
     total_numer = count_note[0] + count_note[1]
     for copy in note_copies:
@@ -798,8 +810,8 @@
             dma((9,)),
             dma((2 * CH, 5)),
             dma((2 * CH, 5)),
-            dma((2, 9)),
-            dma((2, 9)),
+            dma((2, 12)),
+            dma((2, 12)),
             dma((4,)),
             dma((4,)),
         ],

time: 147 us -> 147 us (level)
  no operation moved by 1% of the time
where the time goes in v5:
time: 147 us
  Pallas kernels  145 us (99%)
    pallas_call x1, Pallas kernels, body(): pl.pallas_call(kernel, out_shape=(pltpu.VMEM((STATES, CELLS), F32), pltpu...  143 us

profile of v5, /device:TPU:0, one launch (start us, length us, event | category | flops | bytes accessed | tf_op | source)
XLA Modules:
  0.0 146.6 jit_solution(2596962612501277590)
XLA Ops:
  1.3 143.0 %shard_map.149 = (f32[64,19200]{1,0:T(8,128)S(1)}, f32[1,4800]{1,0:T(1,128)S(1)}) custom-call(f32[64,19200]{1,0:T(8,128)} %bitcast.7, s32[1,3]{1,0:T(1,128)} %flips_in.1, s32[1,1]{1,0:T(1,128)} %bitcast.6.numer_in, f32[1,19200]{1,0:T(1,128)} %pot_in.1, f32[64,19200]{1,0:T(8,128)} %bitcast.8, s32[1,64]{1,0:T(1,128)} %ids_in.1, f32[1,512]{1,0:T(1,128)} %bitcast.9, ...), custom_call_target="tpu_custom_call" | custom-call | tf_op jit(solution)/shard_map/pallas_call | solution.py:769
  144.3 2.3 %shard_map.150 = (f32[64,19200]{1,0:T(8,128)}, f32[1,4800]{1,0:T(1,128)}) custom-call(f32[64,19200]{1,0:T(8,128)S(1)} %get-tuple-element.6.held, f32[1,4800]{1,0:T(1,128)S(1)} %get-tuple-element.7.held_dens), custom_call_target="tpu_custom_call" | custom-call | tf_op jit(solution)/shard_map/pallas_call | solution.py:846

commit v6 on v5

--- a/solution.py
+++ b/solution.py
@@ -276,8 +276,8 @@
                 send_y[chunk, face, 3 * piece : 3 * piece + 3] = jnp.where(
                     lane8 < USED, value[3 * piece : 3 * piece + 3], roll(tail, USED - 8 * piece)
                 )
+        copies[1].start()
         copies[0].start()
-        copies[1].start()
         copies[4].start()
         for face, first in ((0, 0), (1, 2 * CY)):
             parts = [
@@ -290,8 +290,8 @@
             send_x[chunk, face] = jnp.where(
                 lane8 < CZ, parts[0], jnp.where(lane8 < 2 * CZ, parts[1], parts[2])
             )
+        copies[3].start()
         copies[2].start()
-        copies[3].start()
 
     def inner_part(phase, chunk):
         turn = CH * phase + chunk

time: 147 us -> 145 us (0.986)
  Pallas kernels: 145 us -> 143 us
    pallas_call x1, Pallas kernels: 143 us -> 141 us  [body(): pl.pallas_call(kernel, out_shape=(pltpu.VMEM((STATES, CELLS), F32), pltpu...]
where the time goes in v6:
time: 145 us
  Pallas kernels  143 us (99%)
    pallas_call x1, Pallas kernels, body(): pl.pallas_call(kernel, out_shape=(pltpu.VMEM((STATES, CELLS), F32), pltpu...  141 us

profile of v6, /device:TPU:0, one launch (start us, length us, event | category | flops | bytes accessed | tf_op | source)
XLA Modules:
  0.0 144.7 jit_solution(12857216377035413368)
XLA Ops:
  1.3 141.0 %shard_map.149 = (f32[64,19200]{1,0:T(8,128)S(1)}, f32[1,4800]{1,0:T(1,128)S(1)}) custom-call(f32[64,19200]{1,0:T(8,128)} %bitcast.7, s32[1,3]{1,0:T(1,128)} %flips_in.1, s32[1,1]{1,0:T(1,128)} %bitcast.6.numer_in, f32[1,19200]{1,0:T(1,128)} %pot_in.1, f32[64,19200]{1,0:T(8,128)} %bitcast.8, s32[1,64]{1,0:T(1,128)} %ids_in.1, f32[1,512]{1,0:T(1,128)} %bitcast.9, ...), custom_call_target="tpu_custom_call" | custom-call | tf_op jit(solution)/shard_map/pallas_call | solution.py:769
  142.3 2.3 %shard_map.150 = (f32[64,19200]{1,0:T(8,128)}, f32[1,4800]{1,0:T(1,128)}) custom-call(f32[64,19200]{1,0:T(8,128)S(1)} %get-tuple-element.6.held, f32[1,4800]{1,0:T(1,128)S(1)} %get-tuple-element.7.held_dens), custom_call_target="tpu_custom_call" | custom-call | tf_op jit(solution)/shard_map/pallas_call | solution.py:846
